TPU v7x, 512 devices: a whole 4x4x16 slice. The times are simulated.
512 devices in a mesh: tx: 4 (over y), ty: 8 (over x, core), depth: 16 (over z).
Axes of the slice: x: 4, y: 4, z: 16, core: 2. Of those that a mesh axis runs over, the one named last changes fastest.
Arguments:
- volume: bfloat16 [512, 2048, 512], P('depth', 'ty', 'tx'), may hold values from -6 to 6
- transfer: float32 [4, 2], replicated, may hold values from -1.5 to 1.5
- ray_start: int32 [16, 2048, 512], P('depth', 'ty', 'tx'), may hold values from 0 to 15
- ray_stop: int32 [16, 2048, 512], P('depth', 'ty', 'tx'), may hold values from 16 to 32
- pattern: int32 [16, 256, 4], P('depth', 'ty', 'tx'), may hold values 0 or 1
- depth_order: int32 [16], replicated, may hold values from 0 to 15, each once
Outputs:
- frame: float32 [4, 2048, 512], P(None, 'ty', 'tx')
Inputs may be any that keep to these rules, and one draw needn't show every extreme that they name: ray_start[s] < ray_stop[s] for every ray and slice. `depth_order`: each slice appears once.
All inputs are finite; a program needn't handle non-finite values. No bound on the sum of `pattern` on one device may be relied on, other than what follows from the above.
Results may differ from a plain program's by a relative error of at most 0.0003.
Values may be sent and summed in bfloat16 or wider, within the bound.
No kernel may reach another device: no remote copies, remote signals or barrier semaphores. Data moves between devices by JAX's collectives and lax.ppermute only.
A program may use at most 64 MiB of HBM per device.

v0:
```python
import jax
import jax.numpy as jnp
from jax import lax
from jax.sharding import PartitionSpec as P


def extended(array, sides, width):
    edges = {}
    for axis, dim in sides:
        count, length = (lax.axis_size(axis), array.shape[dim])
        up = [(i, (i + 1) % count) for i in range(count - 1)]
        last = lax.slice_in_dim(array, length - width, length, axis=dim)
        initial = lax.slice_in_dim(array, 0, width, axis=dim)
        edges[dim] = (
            lax.ppermute(last, axis, up),
            lax.ppermute(initial, axis, [(b, a) for a, b in up]),
        )
    done = []
    for _, dim in sides:
        low, high = edges[dim]
        around = [(width, width) if d in done else (0, 0) for d in range(array.ndim)]
        array = jnp.concatenate([jnp.pad(low, around), array, jnp.pad(high, around)], axis=dim)
        done.append(dim)
    return array


def local_partial(padded, transfer, ray_start, ray_stop, pattern, depth_count):
    samples = padded.shape[0] - 2
    values = padded[1:-1, 1:-1, 1:-1]
    grad_z = (padded[2:, 1:-1, 1:-1] - padded[:-2, 1:-1, 1:-1]) * 0.5
    grad_y = (padded[1:-1, 2:, 1:-1] - padded[1:-1, :-2, 1:-1]) * 0.5
    grad_x = (padded[1:-1, 1:-1, 2:] - padded[1:-1, 1:-1, :-2]) * 0.5
    lit = jnp.abs(0.48 * grad_x + 0.6 * grad_y + 0.64 * grad_z)
    shading = 0.3 + 0.7 * lit / jnp.sqrt(grad_x * grad_x + grad_y * grad_y + grad_z * grad_z + 1.0)
    rows_each = ray_start.shape[0] // pattern.shape[0]
    cols_each = ray_start.shape[1] // pattern.shape[1]
    pattern_full = jnp.repeat(jnp.repeat(pattern, rows_each, axis=0), cols_each, axis=1)
    layers = lax.broadcasted_iota(jnp.int32, (samples, 1, 1), 0)
    active = (layers >= ray_start[None]) & (layers < ray_stop[None]) & (pattern_full[None] > 0)
    density = jax.nn.softplus(transfer[3, 0] * values + transfer[3, 1]) * (
        2.0 / (samples * depth_count)
    )
    opacity = jnp.where(active, 1.0 - jnp.exp(-density), jnp.float32(0.0))
    passed = jnp.cumprod(1.0 - opacity, axis=0)
    prior = jnp.concatenate([jnp.ones_like(passed[:1]), passed[:-1]], axis=0)
    weights = prior * opacity * shading
    tinted = jax.nn.sigmoid(
        transfer[:3, 0][:, None, None, None] * values[None] + transfer[:3, 1][:, None, None, None]
    )
    colors = jnp.sum(weights[None] * tinted, axis=1)
    return jnp.concatenate([colors, passed[-1][None]], axis=0)


def composite(partials, depth_order):
    count = partials.shape[0]

    def step(position, state_pair):
        colors, remain = state_pair
        slice_part = lax.dynamic_index_in_dim(partials, depth_order[position], 0, keepdims=False)
        return (colors + remain[None] * slice_part[:3], remain * slice_part[3])

    start_pair = (
        jnp.zeros((3,) + partials.shape[2:], jnp.float32),
        jnp.ones(partials.shape[2:], jnp.float32),
    )
    colors, remain = lax.fori_loop(0, count, step, start_pair)
    return jnp.concatenate([colors, 1.0 - remain[None]], axis=0)


def shards(volume, transfer, ray_start, ray_stop, pattern, depth_order):
    padded = extended(volume, (("tx", 2), ("ty", 1), ("depth", 0)), 1).astype(jnp.float32)
    depth_count = lax.axis_size("depth")
    stacked = local_partial(padded, transfer, ray_start[0], ray_stop[0], pattern[0], depth_count)[
        None
    ]
    pixel_share = lax.all_to_all(stacked, "depth", split_axis=2, concat_axis=0, tiled=True)
    picture = composite(pixel_share, depth_order)
    return lax.all_gather(picture, "depth", axis=1, tiled=True)


def solution(mesh):
    in_specs = (
        P("depth", "ty", "tx"),
        P(),
        P("depth", "ty", "tx"),
        P("depth", "ty", "tx"),
        P("depth", "ty", "tx"),
        P(),
    )
    out_specs = P(None, "ty", "tx")
    return jax.shard_map(shards, mesh=mesh, in_specs=in_specs, out_specs=out_specs, check_vma=False)
```

profile of v0, /device:TPU:24, one launch (start us, length us, event | category | flops | bytes accessed | tf_op | source)
XLA Modules:
  0.0 199.9 jit_solution(10582260819200057759)
XLA Ops:
  0.0 0.9 fusion.31
  0.9 1.7 collective-permute-start.1
  2.7 1.3 collective-permute-start.4
  4.0 0.9 fusion.30
  4.8 3.8 %collective-permute-start = (bf16[1,256,128]{2,1,0:T(8,128)(2,1)S(1)}, bf16[1,256,128]{2,1,0:T(8,128)(2,1)S(1)}, u32[]{:S(2)}, u32[]{:S(2)}) collective-permute-start(bf16[1,256,128]{2,1,0:T(8,128)(2,1)S(1)} %get-tuple-element.151), channel_id=1, source_target_pairs={{0,1},{1,2},{2,3},{3,4},{4,5},{5,6},{6,7},{7,8},{8,9},{9,10},{10,1... | collective-permute-start | bytes 196616 | tf_op jit(solution)/shard_map/ppermute | solution.py:15
  8.7 0.0 copy-start.2
  8.7 0.0 copy-start.3
  8.7 1.3 collective-permute-start.5
  10.0 4.4 %fusion.29 = (bf16[32,256,1]{2,1,0:T(8,128)(2,1)}, bf16[32,256,1]{2,1,0:T(8,128)(2,1)S(1)}) fusion(bf16[32,256,128]{2,1,0:T(8,128)(2,1)} %param.8), kind=kLoop, calls=%fused_computation.52 | loop fusion | bytes 65536 | tf_op jit(solution)/shard_map/slice | solution.py:12
  14.4 2.0 copy.23
  16.3 1.3 collective-permute-start.2
  17.7 0.9 copy.24
  18.6 3.4 %collective-permute-done.2 = bf16[32,256,1]{1,0,2:T(8,128)(2,1)S(1)} collective-permute-done((bf16[32,256,1]{1,0,2:T(8,128)(2,1)S(1)}, bf16[32,256,1]{1,0,2:T(8,128)(2,1)S(1)}, u32[]{:S(2)}, u32[]{:S(2)}) %collective-permute-start.2) | collective-permute-done | bytes 16416 | tf_op jit(solution)/shard_map/ppermute | solution.py:15
  22.0 2.6 %collective-permute-start.3 = (bf16[32,256,1]{1,0,2:T(8,128)(2,1)S(1)}, bf16[32,256,1]{1,0,2:T(8,128)(2,1)S(1)}, u32[]{:S(2)}, u32[]{:S(2)}) collective-permute-start(bf16[32,256,1]{1,0,2:T(8,128)(2,1)S(1)} %copy.24), channel_id=1, source_target_pairs={{128,0},{256,128},{384,256},{129,1},{257,129},{385,257},{130,2},{2... | collective-permute-start | bytes 49160 | tf_op jit(solution)/shard_map/ppermute | solution.py:16
  24.6 0.7 fusion.32
  25.3 0.1 broadcast_in_dim.24
  25.3 0.1 gt.22
  25.4 1.9 copy.17
  27.3 1.8 copy.18
  29.2 0.0 collective-permute-done.1
  29.2 17.7 %fusion.11 = f32[34,258,130]{2,1,0:T(8,128)S(1)} fusion(bf16[1,256,128]{2,1,0:T(8,128)(2,1)S(1)} %collective-permute-done.5, bf16[32,1,128]{2,1,0:T(2,128)(2,1)S(1)} %collective-permute-done.4, bf16[32,1,128]{2,1,0:T(2,128)(2,1)S(1)} %collective-permute-done.1, bf16[1,256,128]{2,1,0:T(8,128)(2,1)S(1)} %collective-permute-done, bf16[32,256,1]{2,1,0:T(8,128)(2,1)} %copy.18, ...), kind=kLoop, calls=%fused_computation.23 | loop fusion | flops 33070440 | bytes 6838816 | tf_op jit(solution)/shard_map/convert_element_type | solution.py:71
  46.9 7.6 %fusion.22 = f32[32,256,128]{2,1,0:T(8,128)} fusion(f32[]{:T(128)} %bitcast.4, f32[]{:T(128)} %bitcast.3, s32[256,128]{1,0:T(8,128)S(1)} %bitcast.41, s32[256,128]{1,0:T(8,128)S(1)} %bitcast.43, pred[256]{0:T(512)(128)(4,1)S(1)} %gt.22, f32[34,258,130]{2,1,0:T(8,128)S(1)} %fusion.11), kind=kOutput, calls=%fused_computation.38 | output fusion | flops 50331648 | bytes 8651272 | tf_op jit(solution)/shard_map/jit(cumprod)/reduce_window | solution.py:44
  54.5 4.5 %slice.100 = f32[31,256,128]{2,1,0:T(8,128)} slice(f32[32,256,128]{2,1,0:T(8,128)} %fusion.22), slice={[0:31], [0:256], [0:128]} | slice | bytes 8126464 | tf_op jit(solution)/shard_map/slice | solution.py:45
  59.0 13.6 %add_multiply_fusion = (f32[32,256,128]{2,1,0:T(8,128)S(1)}, f32[32,256,128]{2,1,0:T(8,128)S(1)}) fusion(f32[34,258,130]{2,1,0:T(8,128)S(1)} %fusion.11, f32[31,256,128]{2,1,0:T(8,128)} %slice.100, f32[]{:T(128)} %bitcast.4, f32[]{:T(128)} %bitcast.3, pred[256]{0:T(512)(128)(4,1)S(1)} %gt.22, s32[256,128]{1,0:T(8,128)S(1)} %bitcast.42, ...), kind=kLoop, calls=%fused_computation.37 | loop fusion | flops 40894464 | bytes 42074376 | tf_op jit(solution)/shard_map/mul | solution.py:46
  72.6 3.8 %multiply_reduce_fusion = f32[3,256,128]{2,1,0:T(8,128)S(1)} fusion(f32[3]{0:T(128)S(1)} %get-tuple-element.156, f32[32,256,128]{2,1,0:T(8,128)S(1)} %get-tuple-element.148, f32[3]{0:T(128)S(1)} %get-tuple-element.155, f32[32,256,128]{2,1,0:T(8,128)S(1)} %get-tuple-element.147), kind=kLoop, calls=%fused_computation.9 | loop fusion | flops 21921792 | bytes 8781848 | tf_op jit(solution)/shard_map/reduce_sum | solution.py:50
  76.5 0.0 copy-start.4
  76.5 1.1 copy.19
  77.7 17.1 %all-to-all-start = ((f32[1,4,256,128]{3,1,0,2:T(4,128)}), f32[1,4,256,128]{3,1,0,2:T(4,128)S(1)}, u32[]{:S(2)}, u32[]{:S(2)}) async-start(f32[1,4,256,128]{3,1,0,2:T(4,128)} %copy.19), calls=%async_computation | async-start | bytes 1048576 | tf_op jit(solution)/shard_map/all_to_all | solution.py:76
  94.8 29.3 %all-to-all-done = f32[1,4,256,128]{3,1,0,2:T(4,128)S(1)} async-done(((f32[1,4,256,128]{3,1,0,2:T(4,128)}), f32[1,4,256,128]{3,1,0,2:T(4,128)S(1)}, u32[]{:S(2)}, u32[]{:S(2)}) %all-to-all-start) | async-done | bytes 524320 | tf_op jit(solution)/shard_map/all_to_all | solution.py:76
  124.1 41.5 %while.16 = (s32[]{:T(128)}, f32[3,16,128]{2,1,0:T(8,128)S(1)}, f32[16,128]{1,0:T(8,128)S(1)}, s32[16]{0:T(128)S(1)}, f32[16,4,16,128]{3,2,0,1:T(8,128)S(1)}, /*index=5*/s32[]{:T(128)}, s32[]{:T(128)}, s32[]{:T(128)}) while((s32[]{:T(128)}, f32[3,16,128]{2,1,0:T(8,128)S(1)}, f32[16,128]{1,0:T(8,128)S(1)}, s32[16]{0:T(128)S(1)}, ...), condition=%wide.region_3.4_spmd.clone, body=%wide.region_2.3_spmd.clone.sunk | while | flops 22534 | bytes 180378 | solution.py:66
  124.2 0.6 dynamic_slice.21
  126.8 0.6 dynamic_slice.21
  129.4 0.6 dynamic_slice.21
  131.9 0.6 dynamic_slice.21
  134.5 0.6 dynamic_slice.21
  137.1 0.6 dynamic_slice.21
  139.7 0.6 dynamic_slice.21
  142.3 0.6 dynamic_slice.21
  144.9 0.6 dynamic_slice.21
  147.5 0.6 dynamic_slice.21
  150.1 0.6 dynamic_slice.21
  152.7 0.6 dynamic_slice.21
  155.3 0.6 dynamic_slice.21
  157.9 0.6 dynamic_slice.21
  160.5 0.6 dynamic_slice.21
  163.1 0.6 dynamic_slice.21
  165.7 33.5 %all_gather.3 = f32[4,256,128]{2,1,0:T(8,128)S(1)} all-gather(f32[4,16,128]{2,1,0:T(8,128)S(1)} %pad_maximum_fusion), channel_id=1, replica_groups=mesh['tx'=4,'ty'=8,'depth'=16] {'depth'}, dimensions={1}, use_global_device_ids=true | all-gather | bytes 557056 | tf_op jit(solution)/shard_map/all_gather | solution.py:78
  199.2 0.8 copy.35
  (69 shorter events, 0.5 us)
Async XLA Ops:
  0.9 28.3 %collective-permute-start.1 = (bf16[32,1,128]{2,1,0:T(2,128)(2,1)S(1)}, bf16[32,1,128]{2,1,0:T(2,128)(2,1)S(1)}, u32[]{:S(2)}, u32[]{:S(2)}) collective-permute-start(bf16[32,1,128]{2,1,0:T(2,128)(2,1)S(1)} %get-tuple-element.153), channel_id=1, source_target_pairs={{0,16},{16,32},{32,48},{48,64},{64,80},{80,96},{96,112},{1,17},{17... | collective-permute-start | bytes 24584 | tf_op jit(solution)/shard_map/ppermute | solution.py:15
  2.7 26.5 %collective-permute-start.4 = (bf16[32,1,128]{2,1,0:T(2,128)(2,1)S(1)}, bf16[32,1,128]{2,1,0:T(2,128)(2,1)S(1)}, u32[]{:S(2)}, u32[]{:S(2)}) collective-permute-start(bf16[32,1,128]{2,1,0:T(2,128)(2,1)S(1)} %get-tuple-element.154), channel_id=1, source_target_pairs={{16,0},{32,16},{48,32},{64,48},{80,64},{96,80},{112,96},{17,1},{33... | collective-permute-start | bytes 24584 | tf_op jit(solution)/shard_map/ppermute | solution.py:16
  4.8 24.3 %collective-permute-start = (bf16[1,256,128]{2,1,0:T(8,128)(2,1)S(1)}, bf16[1,256,128]{2,1,0:T(8,128)(2,1)S(1)}, u32[]{:S(2)}, u32[]{:S(2)}) collective-permute-start(bf16[1,256,128]{2,1,0:T(8,128)(2,1)S(1)} %get-tuple-element.151), channel_id=1, source_target_pairs={{0,1},{1,2},{2,3},{3,4},{4,5},{5,6},{6,7},{7,8},{8,9},{9,10},{10,1... | collective-permute-start | bytes 196616 | tf_op jit(solution)/shard_map/ppermute | solution.py:15
  8.7 9.0 %copy-start.2 = (f32[4,2]{0,1:T(2,128)S(1)}, f32[4,2]{0,1:T(2,128)}, u32[]{:S(2)}) copy-start(f32[4,2]{0,1:T(2,128)} %param.9) | copy-start | bytes 100
  8.7 9.0 %copy-start.3 = (s32[1,32,1]{1,2,0:T(1,128)S(1)}, s32[1,32,1]{1,2,0:T(1,128)}, u32[]{:S(2)}) copy-start(s32[1,32,1]{1,2,0:T(1,128)} %param.12) | copy-start | bytes 388
  8.7 20.5 %collective-permute-start.5 = (bf16[1,256,128]{2,1,0:T(8,128)(2,1)S(1)}, bf16[1,256,128]{2,1,0:T(8,128)(2,1)S(1)}, u32[]{:S(2)}, u32[]{:S(2)}) collective-permute-start(bf16[1,256,128]{2,1,0:T(8,128)(2,1)S(1)} %get-tuple-element.152), channel_id=1, source_target_pairs={{1,0},{2,1},{3,2},{4,3},{5,4},{6,5},{7,6},{8,7},{9,8},{10,9},{11,1... | collective-permute-start | bytes 196616 | tf_op jit(solution)/shard_map/ppermute | solution.py:16
  16.3 5.6 %collective-permute-start.2 = (bf16[32,256,1]{1,0,2:T(8,128)(2,1)S(1)}, bf16[32,256,1]{1,0,2:T(8,128)(2,1)S(1)}, u32[]{:S(2)}, u32[]{:S(2)}) collective-permute-start(bf16[32,256,1]{1,0,2:T(8,128)(2,1)S(1)} %copy.23), channel_id=1, source_target_pairs={{0,128},{128,256},{256,384},{1,129},{129,257},{257,385},{2,130},{1... | collective-permute-start | bytes 49160 | tf_op jit(solution)/shard_map/ppermute | solution.py:15
  22.0 5.4 %collective-permute-start.3 = (bf16[32,256,1]{1,0,2:T(8,128)(2,1)S(1)}, bf16[32,256,1]{1,0,2:T(8,128)(2,1)S(1)}, u32[]{:S(2)}, u32[]{:S(2)}) collective-permute-start(bf16[32,256,1]{1,0,2:T(8,128)(2,1)S(1)} %copy.24), channel_id=1, source_target_pairs={{128,0},{256,128},{384,256},{129,1},{257,129},{385,257},{130,2},{2... | collective-permute-start | bytes 49160 | tf_op jit(solution)/shard_map/ppermute | solution.py:16
  29.2 17.7 %copy-start = (s32[1,256,128]{2,1,0:T(8,128)S(1)}, s32[1,256,128]{2,1,0:T(8,128)}, u32[]{:S(2)}) copy-start(s32[1,256,128]{2,1,0:T(8,128)} %param.11) | copy-start | bytes 393220
  29.2 17.7 %copy-start.1 = (s32[1,256,128]{2,1,0:T(8,128)S(1)}, s32[1,256,128]{2,1,0:T(8,128)}, u32[]{:S(2)}) copy-start(s32[1,256,128]{2,1,0:T(8,128)} %param.10) | copy-start | bytes 393220
  72.6 3.8 %slice-start = ((f32[32,256,128]{2,1,0:T(8,128)}), f32[1,256,128]{2,1,0:T(8,128)S(1)}, s32[]{:S(2)}) async-start(f32[32,256,128]{2,1,0:T(8,128)} %fusion.22), calls=%async_computation.1 | async-start | bytes 262144 | tf_op jit(solution)/shard_map/slice | solution.py:51
  76.5 47.7 %copy-start.4 = (s32[16]{0:T(128)S(1)}, s32[16]{0:T(128)}, u32[]{:S(2)}) copy-start(s32[16]{0:T(128)} %param.13) | copy-start | bytes 196
  77.7 46.4 %all-to-all-start = ((f32[1,4,256,128]{3,1,0,2:T(4,128)}), f32[1,4,256,128]{3,1,0,2:T(4,128)S(1)}, u32[]{:S(2)}, u32[]{:S(2)}) async-start(f32[1,4,256,128]{3,1,0,2:T(4,128)} %copy.19), calls=%async_computation | async-start | bytes 1048576 | tf_op jit(solution)/shard_map/all_to_all | solution.py:76
where the time goes:
time: 201 us; the launch traced here: 200 us
  other arithmetic  43 us (21%)
  blocking collectives  33.5 us (17%)
  waiting for transfers between devices  32.7 us (16%)
  loops' own time  31.7 us (16%)
  local copies, waits for them, and re-layouts  29.6 us (15%)
  starting transfers between devices  29.2 us (15%)
    all_gather x1, blocking collectives, shards(): return lax.all_gather(picture, 'depth', axis=1, tiled=True)  33.5 us
    another operation x1, loops' own time, composite(): colors, remain = lax.fori_loop(0, count, step, start_pair)  31.7 us
    all_to_all x1, waiting for transfers between devices, shards(): lax.all_to_all(stacked, 'depth', split_axis=2, concat_axis=0, tiled=True)  29.3 us
    convert_element_type x1, other arithmetic, shards(): extended(volume, (('tx', 2), ('ty', 1), ('depth', 0)), 1)  17.7 us
    all_to_all x1, starting transfers between devices, shards(): lax.all_to_all(stacked, 'depth', split_axis=2, concat_axis=0, tiled=True)  17.1 us
    mul x1, other arithmetic, local_partial(): weights = prior * opacity * shading  13.6 us
    dynamic_slice x16, local copies, waits for them, and re-layouts, step(): depth_order[position]  9.38 us
    another operation x1, other arithmetic, local_partial(): passed = jnp.cumprod(1.0 - opacity, axis=0)  7.63 us
  transfers between devices with their start and end apart: 7, of which 2 were waited for; matrix products, arithmetic and copies ran while one was open for 6% of the time, Pallas kernels for 0%

commit v1 on v0

--- a/solution.py
+++ b/solution.py
@@ -75,7 +75,36 @@
     ]
     pixel_share = lax.all_to_all(stacked, "depth", split_axis=2, concat_axis=0, tiled=True)
     picture = composite(pixel_share, depth_order)
-    return lax.all_gather(picture, "depth", axis=1, tiled=True)
+
+    def watch_desk(in_array):
+        val2 = lax.axis_size("depth")
+        x_next = lax.axis_index("depth")
+        work_now, a_next, local_out = (val2, x_next, in_array.shape[1])
+        all_rows = []
+        for jj, idx in enumerate(in_array.shape):
+            all_rows.append(idx * work_now if jj == 1 else idx)
+        f_now = jnp.zeros(all_rows, in_array.dtype)
+        w1 = lax.dynamic_update_slice_in_dim(f_now, in_array, a_next * local_out, axis=1)
+        g_now = z = in_array
+        for t in range(1, work_now // 2 + 1):
+            fields = []
+            for jj in range(work_now):
+                fields.append((jj, (jj + 1) % work_now))
+            g_now = lax.ppermute(g_now, "depth", fields)
+            w1 = lax.dynamic_update_slice_in_dim(
+                w1, g_now, (a_next - t) % work_now * local_out, axis=1
+            )
+            if 2 * t < work_now:
+                all_blocks = []
+                for jj in range(work_now):
+                    all_blocks.append((jj, (jj - 1) % work_now))
+                z = lax.ppermute(z, "depth", all_blocks)
+                w1 = lax.dynamic_update_slice_in_dim(
+                    w1, z, (a_next + t) % work_now * local_out, axis=1
+                )
+        return w1
+
+    return watch_desk(picture)
 
 
 def solution(mesh):

time: 201 us -> 227 us (1.13); the launches traced: 200 us -> 223 us
  starting transfers between devices: 29.2 us -> 82.2 us
  blocking collectives: 33.5 us -> 0 us
  waiting for transfers between devices: 32.7 us -> 35.5 us
    ppermute x0 -> x15, starting transfers between devices: none -> 53 us  [the longest x7 35.6 us: watch_desk(): z = lax.ppermute(z, 'depth', all_blocks)]
    all_gather x1 -> x0, blocking collectives: 33.5 us -> none  [shards(): return lax.all_gather(picture, 'depth', axis=1, tiled=True)]
    ppermute x0 -> x15, waiting for transfers between devices: none -> 5.21 us  [the longest x8 5.19 us: watch_desk(): g_now = lax.ppermute(g_now, 'depth', fields)]
  transfers between devices with their start and end apart: 7 -> 22, of which waited for: 2 -> 5; matrix products, arithmetic and copies ran while one was open for 6% -> 6% of each run, Pallas kernels for 0% -> 0%
where the time goes in v1:
time: 227 us; the launch traced here: 223 us
  starting transfers between devices  82.2 us (36%)
  other arithmetic  43 us (19%)
  waiting for transfers between devices  35.5 us (16%)
  loops' own time  31.8 us (14%)
  local copies, waits for them, and re-layouts  29.7 us (13%)
    ppermute x7, starting transfers between devices, watch_desk(): z = lax.ppermute(z, 'depth', all_blocks)  35.6 us
    another operation x1, loops' own time, composite(): colors, remain = lax.fori_loop(0, count, step, start_pair)  31.8 us
    all_to_all x1, waiting for transfers between devices, shards(): lax.all_to_all(stacked, 'depth', split_axis=2, concat_axis=0, tiled=True)  27.9 us
    convert_element_type x1, other arithmetic, shards(): extended(volume, (('tx', 2), ('ty', 1), ('depth', 0)), 1)  17.7 us
    ppermute x8, starting transfers between devices, watch_desk(): g_now = lax.ppermute(g_now, 'depth', fields)  17.4 us
    all_to_all x1, starting transfers between devices, shards(): lax.all_to_all(stacked, 'depth', split_axis=2, concat_axis=0, tiled=True)  15.2 us
    mul x1, other arithmetic, local_partial(): weights = prior * opacity * shading  13.6 us
    dynamic_slice x16, local copies, waits for them, and re-layouts, step(): depth_order[position]  9.38 us
  transfers between devices with their start and end apart: 22, of which 5 were waited for; matrix products, arithmetic and copies ran while one was open for 6% of the time, Pallas kernels for 0%

profile of v1, /device:TPU:24, one launch (start us, length us, event | category | flops | bytes accessed | tf_op | source)
XLA Modules:
  0.0 223.2 jit_solution(13624926779371231949)
XLA Ops:
  0.0 0.9 fusion.30
  0.9 1.3 collective-permute-start.5
  2.2 0.9 fusion.31
  3.1 1.3 collective-permute-start.4
  4.4 3.0 %collective-permute-start.1 = (bf16[32,1,128]{2,1,0:T(2,128)(2,1)S(1)}, bf16[32,1,128]{2,1,0:T(2,128)(2,1)S(1)}, u32[]{:S(2)}, u32[]{:S(2)}) collective-permute-start(bf16[32,1,128]{2,1,0:T(2,128)(2,1)S(1)} %get-tuple-element.153), channel_id=1, source_target_pairs={{0,16},{16,32},{32,48},{48,64},{64,80},{80,96},{96,112},{1,17},{17... | collective-permute-start | bytes 24584 | tf_op jit(solution)/shard_map/ppermute | solution.py:15
  7.5 4.5 %collective-permute-start = (bf16[1,256,128]{2,1,0:T(8,128)(2,1)S(1)}, bf16[1,256,128]{2,1,0:T(8,128)(2,1)S(1)}, u32[]{:S(2)}, u32[]{:S(2)}) collective-permute-start(bf16[1,256,128]{2,1,0:T(8,128)(2,1)S(1)} %get-tuple-element.151), channel_id=1, source_target_pairs={{0,1},{1,2},{2,3},{3,4},{4,5},{5,6},{6,7},{7,8},{8,9},{9,10},{10,1... | collective-permute-start | bytes 196616 | tf_op jit(solution)/shard_map/ppermute | solution.py:15
  12.0 4.5 %fusion.29 = (bf16[32,256,1]{2,1,0:T(8,128)(2,1)S(1)}, bf16[32,256,1]{2,1,0:T(8,128)(2,1)}) fusion(bf16[32,256,128]{2,1,0:T(8,128)(2,1)} %param.8), kind=kLoop, calls=%fused_computation.68 | loop fusion | bytes 65536 | tf_op jit(solution)/shard_map/slice | solution.py:12
  16.5 2.0 copy.24
  18.4 2.6 %collective-permute-start.3 = (bf16[32,256,1]{1,0,2:T(8,128)(2,1)S(1)}, bf16[32,256,1]{1,0,2:T(8,128)(2,1)S(1)}, u32[]{:S(2)}, u32[]{:S(2)}) collective-permute-start(bf16[32,256,1]{1,0,2:T(8,128)(2,1)S(1)} %copy.24), channel_id=1, source_target_pairs={{128,0},{256,128},{384,256},{129,1},{257,129},{385,257},{130,2},{2... | collective-permute-start | bytes 49160 | tf_op jit(solution)/shard_map/ppermute | solution.py:16
  21.1 0.9 copy.23
  22.5 1.3 collective-permute-start.2
  23.8 0.7 fusion.32
  24.6 1.8 copy.18
  26.5 2.0 collective-permute-done.2
  28.5 1.8 copy.17
  30.3 17.7 %fusion.11 = f32[34,258,130]{2,1,0:T(8,128)S(1)} fusion(bf16[1,256,128]{2,1,0:T(8,128)(2,1)S(1)} %collective-permute-done.5, bf16[32,1,128]{2,1,0:T(2,128)(2,1)S(1)} %collective-permute-done.4, bf16[32,1,128]{2,1,0:T(2,128)(2,1)S(1)} %collective-permute-done.1, bf16[1,256,128]{2,1,0:T(8,128)(2,1)S(1)} %collective-permute-done, bf16[32,256,1]{2,1,0:T(8,128)(2,1)} %copy.18, ...), kind=kLoop, calls=%fused_computation.23 | loop fusion | flops 33070440 | bytes 6838816 | tf_op jit(solution)/shard_map/convert_element_type | solution.py:71
  48.0 7.7 %fusion.22 = f32[32,256,128]{2,1,0:T(8,128)} fusion(f32[]{:T(128)} %bitcast.4, f32[]{:T(128)} %bitcast.3, s32[256,128]{1,0:T(8,128)S(1)} %bitcast.41, s32[256,128]{1,0:T(8,128)S(1)} %bitcast.43, pred[256]{0:T(512)(128)(4,1)S(1)} %gt.22, f32[34,258,130]{2,1,0:T(8,128)S(1)} %fusion.11), kind=kOutput, calls=%fused_computation.38 | output fusion | flops 50331648 | bytes 8651272 | tf_op jit(solution)/shard_map/jit(cumprod)/reduce_window | solution.py:44
  55.7 4.6 %slice.100 = f32[31,256,128]{2,1,0:T(8,128)} slice(f32[32,256,128]{2,1,0:T(8,128)} %fusion.22), slice={[0:31], [0:256], [0:128]} | slice | bytes 8126464 | tf_op jit(solution)/shard_map/slice | solution.py:45
  60.2 13.6 %add_multiply_fusion = (f32[32,256,128]{2,1,0:T(8,128)S(1)}, f32[32,256,128]{2,1,0:T(8,128)S(1)}) fusion(f32[34,258,130]{2,1,0:T(8,128)S(1)} %fusion.11, f32[31,256,128]{2,1,0:T(8,128)} %slice.100, f32[]{:T(128)} %bitcast.4, f32[]{:T(128)} %bitcast.3, pred[256]{0:T(512)(128)(4,1)S(1)} %gt.22, s32[256,128]{1,0:T(8,128)S(1)} %bitcast.42, ...), kind=kLoop, calls=%fused_computation.37 | loop fusion | flops 40894464 | bytes 42074376 | tf_op jit(solution)/shard_map/mul | solution.py:46
  73.8 3.8 %multiply_reduce_fusion = f32[3,256,128]{2,1,0:T(8,128)S(1)} fusion(f32[3]{0:T(128)S(1)} %get-tuple-element.158, f32[32,256,128]{2,1,0:T(8,128)S(1)} %get-tuple-element.148, f32[3]{0:T(128)S(1)} %get-tuple-element.157, f32[32,256,128]{2,1,0:T(8,128)S(1)} %get-tuple-element.147), kind=kLoop, calls=%fused_computation.9 | loop fusion | flops 21921792 | bytes 8781848 | tf_op jit(solution)/shard_map/reduce_sum | solution.py:50
  77.7 1.1 copy.19
  78.9 15.2 %all-to-all-start = ((f32[1,4,256,128]{3,1,0,2:T(4,128)}), f32[1,4,256,128]{3,1,0,2:T(4,128)S(1)}, u32[]{:S(2)}, u32[]{:S(2)}) async-start(f32[1,4,256,128]{3,1,0,2:T(4,128)} %copy.19), calls=%async_computation | async-start | bytes 1048576 | tf_op jit(solution)/shard_map/all_to_all | solution.py:76
  94.1 27.9 %all-to-all-done = f32[1,4,256,128]{3,1,0,2:T(4,128)S(1)} async-done(((f32[1,4,256,128]{3,1,0,2:T(4,128)}), f32[1,4,256,128]{3,1,0,2:T(4,128)S(1)}, u32[]{:S(2)}, u32[]{:S(2)}) %all-to-all-start) | async-done | bytes 524320 | tf_op jit(solution)/shard_map/all_to_all | solution.py:76
  122.0 41.5 %while.16 = (s32[]{:T(128)}, f32[3,16,128]{2,1,0:T(8,128)S(1)}, f32[16,128]{1,0:T(8,128)S(1)}, s32[16]{0:T(128)S(1)}, f32[16,4,16,128]{3,2,0,1:T(8,128)S(1)}, /*index=5*/s32[]{:T(128)}, s32[]{:T(128)}, s32[]{:T(128)}) while((s32[]{:T(128)}, f32[3,16,128]{2,1,0:T(8,128)S(1)}, f32[16,128]{1,0:T(8,128)S(1)}, s32[16]{0:T(128)S(1)}, ...), condition=%wide.region_3.4_spmd.clone, body=%wide.region_2.3_spmd.clone.sunk | while | flops 22534 | bytes 180378 | solution.py:66
  122.0 0.6 dynamic_slice.21
  124.6 0.6 dynamic_slice.21
  127.2 0.6 dynamic_slice.21
  129.8 0.6 dynamic_slice.21
  132.4 0.6 dynamic_slice.21
  135.0 0.6 dynamic_slice.21
  142.8 0.6 dynamic_slice.21
  163.6 3.9 %collective-permute-start.6 = (f32[4,16,128]{2,1,0:T(8,128)S(1)}, f32[4,16,128]{2,1,0:T(8,128)S(1)}, u32[]{:S(2)}, u32[]{:S(2)}) collective-permute-start(f32[4,16,128]{2,1,0:T(8,128)S(1)} %get-tuple-element.155), channel_id=1, source_target_pairs={{0,1},{1,2},{2,3},{3,4},{4,5},{5,6},{6,7},{7,8},{8,9},{9,10},{10,1... | collective-permute-start | bytes 98312 | tf_op jit(solution)/shard_map/ppermute | solution.py:93
  167.6 4.8 %collective-permute-start.7 = (f32[4,16,128]{2,1,0:T(8,128)S(1)}, f32[4,16,128]{2,1,0:T(8,128)S(1)}, u32[]{:S(2)}, u32[]{:S(2)}) collective-permute-start(f32[4,16,128]{2,1,0:T(8,128)S(1)} %get-tuple-element.155), channel_id=1, source_target_pairs={{0,15},{1,0},{2,1},{3,2},{4,3},{5,4},{6,5},{7,6},{8,7},{9,8},{10,9... | collective-permute-start | bytes 98312 | tf_op jit(solution)/shard_map/ppermute | solution.py:101
  172.6 1.9 collective-permute-start.8
  174.6 5.1 %collective-permute-start.9 = (f32[4,16,128]{2,1,0:T(8,128)S(1)}, f32[4,16,128]{2,1,0:T(8,128)S(1)}, u32[]{:S(2)}, u32[]{:S(2)}) collective-permute-start(f32[4,16,128]{2,1,0:T(8,128)S(1)} %collective-permute-done.7), channel_id=1, source_target_pairs={{0,15},{1,0},{2,1},{3,2},{4,3},{5,4},{6,5},{7,6},{8,7},{9,8},{10,9... | collective-permute-start | bytes 98312 | tf_op jit(solution)/shard_map/ppermute | solution.py:101
  179.8 1.9 collective-permute-start.10
  181.7 5.2 %collective-permute-start.11 = (f32[4,16,128]{2,1,0:T(8,128)S(1)}, f32[4,16,128]{2,1,0:T(8,128)S(1)}, u32[]{:S(2)}, u32[]{:S(2)}) collective-permute-start(f32[4,16,128]{2,1,0:T(8,128)S(1)} %collective-permute-done.9), channel_id=1, source_target_pairs={{0,15},{1,0},{2,1},{3,2},{4,3},{5,4},{6,5},{7,6},{8,7},{9,8},{10,9... | collective-permute-start | bytes 98312 | tf_op jit(solution)/shard_map/ppermute | solution.py:101
  187.1 1.9 collective-permute-start.12
  189.0 5.1 %collective-permute-start.13 = (f32[4,16,128]{2,1,0:T(8,128)S(1)}, f32[4,16,128]{2,1,0:T(8,128)S(1)}, u32[]{:S(2)}, u32[]{:S(2)}) collective-permute-start(f32[4,16,128]{2,1,0:T(8,128)S(1)} %collective-permute-done.11), channel_id=1, source_target_pairs={{0,15},{1,0},{2,1},{3,2},{4,3},{5,4},{6,5},{7,6},{8,7},{9,8},{10,9... | collective-permute-start | bytes 98312 | tf_op jit(solution)/shard_map/ppermute | solution.py:101
  194.2 1.9 collective-permute-start.14
  196.1 5.1 %collective-permute-start.15 = (f32[4,16,128]{2,1,0:T(8,128)S(1)}, f32[4,16,128]{2,1,0:T(8,128)S(1)}, u32[]{:S(2)}, u32[]{:S(2)}) collective-permute-start(f32[4,16,128]{2,1,0:T(8,128)S(1)} %collective-permute-done.13), channel_id=1, source_target_pairs={{0,15},{1,0},{2,1},{3,2},{4,3},{5,4},{6,5},{7,6},{8,7},{9,8},{10,9... | collective-permute-start | bytes 98312 | tf_op jit(solution)/shard_map/ppermute | solution.py:101
  201.3 1.9 collective-permute-start.16
  203.2 5.1 %collective-permute-start.17 = (f32[4,16,128]{2,1,0:T(8,128)S(1)}, f32[4,16,128]{2,1,0:T(8,128)S(1)}, u32[]{:S(2)}, u32[]{:S(2)}) collective-permute-start(f32[4,16,128]{2,1,0:T(8,128)S(1)} %collective-permute-done.15), channel_id=1, source_target_pairs={{0,15},{1,0},{2,1},{3,2},{4,3},{5,4},{6,5},{7,6},{8,7},{9,8},{10,9... | collective-permute-start | bytes 98312 | tf_op jit(solution)/shard_map/ppermute | solution.py:101
  208.4 1.9 collective-permute-start.18
  210.4 5.1 %collective-permute-start.19 = (f32[4,16,128]{2,1,0:T(8,128)S(1)}, f32[4,16,128]{2,1,0:T(8,128)S(1)}, u32[]{:S(2)}, u32[]{:S(2)}) collective-permute-start(f32[4,16,128]{2,1,0:T(8,128)S(1)} %collective-permute-done.17), channel_id=1, source_target_pairs={{0,15},{1,0},{2,1},{3,2},{4,3},{5,4},{6,5},{7,6},{8,7},{9,8},{10,9... | collective-permute-start | bytes 98312 | tf_op jit(solution)/shard_map/ppermute | solution.py:101
  215.5 1.9 collective-permute-start.20
  217.5 5.0 %collective-permute-done.20 = f32[4,16,128]{2,1,0:T(8,128)S(1)} collective-permute-done((f32[4,16,128]{2,1,0:T(8,128)S(1)}, f32[4,16,128]{2,1,0:T(8,128)S(1)}, u32[]{:S(2)}, u32[]{:S(2)}) %collective-permute-start.20) | collective-permute-done | bytes 32800 | tf_op jit(solution)/shard_map/ppermute | solution.py:93
  222.6 0.6 constant_dynamic-update-slice_fusion
  (115 shorter events, 6.8 us)
Async XLA Ops:
  0.9 29.4 %collective-permute-start.5 = (bf16[1,256,128]{2,1,0:T(8,128)(2,1)S(1)}, bf16[1,256,128]{2,1,0:T(8,128)(2,1)S(1)}, u32[]{:S(2)}, u32[]{:S(2)}) collective-permute-start(bf16[1,256,128]{2,1,0:T(8,128)(2,1)S(1)} %get-tuple-element.152), channel_id=1, source_target_pairs={{1,0},{2,1},{3,2},{4,3},{5,4},{6,5},{7,6},{8,7},{9,8},{10,9},{11,1... | collective-permute-start | bytes 196616 | tf_op jit(solution)/shard_map/ppermute | solution.py:16
  3.1 27.2 %collective-permute-start.4 = (bf16[32,1,128]{2,1,0:T(2,128)(2,1)S(1)}, bf16[32,1,128]{2,1,0:T(2,128)(2,1)S(1)}, u32[]{:S(2)}, u32[]{:S(2)}) collective-permute-start(bf16[32,1,128]{2,1,0:T(2,128)(2,1)S(1)} %get-tuple-element.154), channel_id=1, source_target_pairs={{16,0},{32,16},{48,32},{64,48},{80,64},{96,80},{112,96},{17,1},{33... | collective-permute-start | bytes 24584 | tf_op jit(solution)/shard_map/ppermute | solution.py:16
  4.4 25.9 %collective-permute-start.1 = (bf16[32,1,128]{2,1,0:T(2,128)(2,1)S(1)}, bf16[32,1,128]{2,1,0:T(2,128)(2,1)S(1)}, u32[]{:S(2)}, u32[]{:S(2)}) collective-permute-start(bf16[32,1,128]{2,1,0:T(2,128)(2,1)S(1)} %get-tuple-element.153), channel_id=1, source_target_pairs={{0,16},{16,32},{32,48},{48,64},{64,80},{80,96},{96,112},{1,17},{17... | collective-permute-start | bytes 24584 | tf_op jit(solution)/shard_map/ppermute | solution.py:15
  7.4 13.7 %copy-start.3 = (f32[4,2]{0,1:T(2,128)S(1)}, f32[4,2]{0,1:T(2,128)}, u32[]{:S(2)}) copy-start(f32[4,2]{0,1:T(2,128)} %param.9) | copy-start | bytes 100
  7.4 13.7 %copy-start.4 = (s32[1,32,1]{1,2,0:T(1,128)S(1)}, s32[1,32,1]{1,2,0:T(1,128)}, u32[]{:S(2)}) copy-start(s32[1,32,1]{1,2,0:T(1,128)} %param.12) | copy-start | bytes 388
  7.5 22.9 %collective-permute-start = (bf16[1,256,128]{2,1,0:T(8,128)(2,1)S(1)}, bf16[1,256,128]{2,1,0:T(8,128)(2,1)S(1)}, u32[]{:S(2)}, u32[]{:S(2)}) collective-permute-start(bf16[1,256,128]{2,1,0:T(8,128)(2,1)S(1)} %get-tuple-element.151), channel_id=1, source_target_pairs={{0,1},{1,2},{2,3},{3,4},{4,5},{5,6},{6,7},{7,8},{8,9},{9,10},{10,1... | collective-permute-start | bytes 196616 | tf_op jit(solution)/shard_map/ppermute | solution.py:15
  18.4 4.1 %collective-permute-start.3 = (bf16[32,256,1]{1,0,2:T(8,128)(2,1)S(1)}, bf16[32,256,1]{1,0,2:T(8,128)(2,1)S(1)}, u32[]{:S(2)}, u32[]{:S(2)}) collective-permute-start(bf16[32,256,1]{1,0,2:T(8,128)(2,1)S(1)} %copy.24), channel_id=1, source_target_pairs={{128,0},{256,128},{384,256},{129,1},{257,129},{385,257},{130,2},{2... | collective-permute-start | bytes 49160 | tf_op jit(solution)/shard_map/ppermute | solution.py:16
  22.5 5.9 %collective-permute-start.2 = (bf16[32,256,1]{1,0,2:T(8,128)(2,1)S(1)}, bf16[32,256,1]{1,0,2:T(8,128)(2,1)S(1)}, u32[]{:S(2)}, u32[]{:S(2)}) collective-permute-start(bf16[32,256,1]{1,0,2:T(8,128)(2,1)S(1)} %copy.23), channel_id=1, source_target_pairs={{0,128},{128,256},{256,384},{1,129},{129,257},{257,385},{2,130},{1... | collective-permute-start | bytes 49160 | tf_op jit(solution)/shard_map/ppermute | solution.py:15
  30.3 17.7 %copy-start = (s32[1,256,128]{2,1,0:T(8,128)S(1)}, s32[1,256,128]{2,1,0:T(8,128)}, u32[]{:S(2)}) copy-start(s32[1,256,128]{2,1,0:T(8,128)} %param.11) | copy-start | bytes 393220
  30.3 17.7 %copy-start.1 = (s32[1,256,128]{2,1,0:T(8,128)S(1)}, s32[1,256,128]{2,1,0:T(8,128)}, u32[]{:S(2)}) copy-start(s32[1,256,128]{2,1,0:T(8,128)} %param.10) | copy-start | bytes 393220
  73.8 3.8 %slice-start = ((f32[32,256,128]{2,1,0:T(8,128)}), f32[1,256,128]{2,1,0:T(8,128)S(1)}, s32[]{:S(2)}) async-start(f32[32,256,128]{2,1,0:T(8,128)} %fusion.22), calls=%async_computation.1 | async-start | bytes 262144 | tf_op jit(solution)/shard_map/slice | solution.py:51
  77.7 44.3 %copy-start.5 = (s32[16]{0:T(128)S(1)}, s32[16]{0:T(128)}, u32[]{:S(2)}) copy-start(s32[16]{0:T(128)} %param.13) | copy-start | bytes 196
  78.9 43.1 %all-to-all-start = ((f32[1,4,256,128]{3,1,0,2:T(4,128)}), f32[1,4,256,128]{3,1,0,2:T(4,128)S(1)}, u32[]{:S(2)}, u32[]{:S(2)}) async-start(f32[1,4,256,128]{3,1,0,2:T(4,128)} %copy.19), calls=%async_computation | async-start | bytes 1048576 | tf_op jit(solution)/shard_map/all_to_all | solution.py:76
  163.6 9.0 %collective-permute-start.6 = (f32[4,16,128]{2,1,0:T(8,128)S(1)}, f32[4,16,128]{2,1,0:T(8,128)S(1)}, u32[]{:S(2)}, u32[]{:S(2)}) collective-permute-start(f32[4,16,128]{2,1,0:T(8,128)S(1)} %get-tuple-element.155), channel_id=1, source_target_pairs={{0,1},{1,2},{2,3},{3,4},{4,5},{5,6},{6,7},{7,8},{8,9},{9,10},{10,1... | collective-permute-start | bytes 98312 | tf_op jit(solution)/shard_map/ppermute | solution.py:93
  167.6 7.0 %collective-permute-start.7 = (f32[4,16,128]{2,1,0:T(8,128)S(1)}, f32[4,16,128]{2,1,0:T(8,128)S(1)}, u32[]{:S(2)}, u32[]{:S(2)}) collective-permute-start(f32[4,16,128]{2,1,0:T(8,128)S(1)} %get-tuple-element.155), channel_id=1, source_target_pairs={{0,15},{1,0},{2,1},{3,2},{4,3},{5,4},{6,5},{7,6},{8,7},{9,8},{10,9... | collective-permute-start | bytes 98312 | tf_op jit(solution)/shard_map/ppermute | solution.py:101
  172.6 7.1 %collective-permute-start.8 = (f32[4,16,128]{2,1,0:T(8,128)S(1)}, f32[4,16,128]{2,1,0:T(8,128)S(1)}, u32[]{:S(2)}, u32[]{:S(2)}) collective-permute-start(f32[4,16,128]{2,1,0:T(8,128)S(1)} %collective-permute-done.6), channel_id=1, source_target_pairs={{0,1},{1,2},{2,3},{3,4},{4,5},{5,6},{6,7},{7,8},{8,9},{9,10},{10,1... | collective-permute-start | bytes 98312 | tf_op jit(solution)/shard_map/ppermute | solution.py:93
  174.6 7.1 %collective-permute-start.9 = (f32[4,16,128]{2,1,0:T(8,128)S(1)}, f32[4,16,128]{2,1,0:T(8,128)S(1)}, u32[]{:S(2)}, u32[]{:S(2)}) collective-permute-start(f32[4,16,128]{2,1,0:T(8,128)S(1)} %collective-permute-done.7), channel_id=1, source_target_pairs={{0,15},{1,0},{2,1},{3,2},{4,3},{5,4},{6,5},{7,6},{8,7},{9,8},{10,9... | collective-permute-start | bytes 98312 | tf_op jit(solution)/shard_map/ppermute | solution.py:101
  179.8 7.3 %collective-permute-start.10 = (f32[4,16,128]{2,1,0:T(8,128)S(1)}, f32[4,16,128]{2,1,0:T(8,128)S(1)}, u32[]{:S(2)}, u32[]{:S(2)}) collective-permute-start(f32[4,16,128]{2,1,0:T(8,128)S(1)} %collective-permute-done.8), channel_id=1, source_target_pairs={{0,1},{1,2},{2,3},{3,4},{4,5},{5,6},{6,7},{7,8},{8,9},{9,10},{10,1... | collective-permute-start | bytes 98312 | tf_op jit(solution)/shard_map/ppermute | solution.py:93
  181.7 7.3 %collective-permute-start.11 = (f32[4,16,128]{2,1,0:T(8,128)S(1)}, f32[4,16,128]{2,1,0:T(8,128)S(1)}, u32[]{:S(2)}, u32[]{:S(2)}) collective-permute-start(f32[4,16,128]{2,1,0:T(8,128)S(1)} %collective-permute-done.9), channel_id=1, source_target_pairs={{0,15},{1,0},{2,1},{3,2},{4,3},{5,4},{6,5},{7,6},{8,7},{9,8},{10,9... | collective-permute-start | bytes 98312 | tf_op jit(solution)/shard_map/ppermute | solution.py:101
  187.1 7.1 %collective-permute-start.12 = (f32[4,16,128]{2,1,0:T(8,128)S(1)}, f32[4,16,128]{2,1,0:T(8,128)S(1)}, u32[]{:S(2)}, u32[]{:S(2)}) collective-permute-start(f32[4,16,128]{2,1,0:T(8,128)S(1)} %collective-permute-done.10), channel_id=1, source_target_pairs={{0,1},{1,2},{2,3},{3,4},{4,5},{5,6},{6,7},{7,8},{8,9},{9,10},{10,1... | collective-permute-start | bytes 98312 | tf_op jit(solution)/shard_map/ppermute | solution.py:93
  189.0 7.1 %collective-permute-start.13 = (f32[4,16,128]{2,1,0:T(8,128)S(1)}, f32[4,16,128]{2,1,0:T(8,128)S(1)}, u32[]{:S(2)}, u32[]{:S(2)}) collective-permute-start(f32[4,16,128]{2,1,0:T(8,128)S(1)} %collective-permute-done.11), channel_id=1, source_target_pairs={{0,15},{1,0},{2,1},{3,2},{4,3},{5,4},{6,5},{7,6},{8,7},{9,8},{10,9... | collective-permute-start | bytes 98312 | tf_op jit(solution)/shard_map/ppermute | solution.py:101
  194.2 7.1 %collective-permute-start.14 = (f32[4,16,128]{2,1,0:T(8,128)S(1)}, f32[4,16,128]{2,1,0:T(8,128)S(1)}, u32[]{:S(2)}, u32[]{:S(2)}) collective-permute-start(f32[4,16,128]{2,1,0:T(8,128)S(1)} %collective-permute-done.12), channel_id=1, source_target_pairs={{0,1},{1,2},{2,3},{3,4},{4,5},{5,6},{6,7},{7,8},{8,9},{9,10},{10,1... | collective-permute-start | bytes 98312 | tf_op jit(solution)/shard_map/ppermute | solution.py:93
  196.1 7.1 %collective-permute-start.15 = (f32[4,16,128]{2,1,0:T(8,128)S(1)}, f32[4,16,128]{2,1,0:T(8,128)S(1)}, u32[]{:S(2)}, u32[]{:S(2)}) collective-permute-start(f32[4,16,128]{2,1,0:T(8,128)S(1)} %collective-permute-done.13), channel_id=1, source_target_pairs={{0,15},{1,0},{2,1},{3,2},{4,3},{5,4},{6,5},{7,6},{8,7},{9,8},{10,9... | collective-permute-start | bytes 98312 | tf_op jit(solution)/shard_map/ppermute | solution.py:101
  201.3 7.1 %collective-permute-start.16 = (f32[4,16,128]{2,1,0:T(8,128)S(1)}, f32[4,16,128]{2,1,0:T(8,128)S(1)}, u32[]{:S(2)}, u32[]{:S(2)}) collective-permute-start(f32[4,16,128]{2,1,0:T(8,128)S(1)} %collective-permute-done.14), channel_id=1, source_target_pairs={{0,1},{1,2},{2,3},{3,4},{4,5},{5,6},{6,7},{7,8},{8,9},{9,10},{10,1... | collective-permute-start | bytes 98312 | tf_op jit(solution)/shard_map/ppermute | solution.py:93
  203.2 7.1 %collective-permute-start.17 = (f32[4,16,128]{2,1,0:T(8,128)S(1)}, f32[4,16,128]{2,1,0:T(8,128)S(1)}, u32[]{:S(2)}, u32[]{:S(2)}) collective-permute-start(f32[4,16,128]{2,1,0:T(8,128)S(1)} %collective-permute-done.15), channel_id=1, source_target_pairs={{0,15},{1,0},{2,1},{3,2},{4,3},{5,4},{6,5},{7,6},{8,7},{9,8},{10,9... | collective-permute-start | bytes 98312 | tf_op jit(solution)/shard_map/ppermute | solution.py:101
  208.4 7.1 %collective-permute-start.18 = (f32[4,16,128]{2,1,0:T(8,128)S(1)}, f32[4,16,128]{2,1,0:T(8,128)S(1)}, u32[]{:S(2)}, u32[]{:S(2)}) collective-permute-start(f32[4,16,128]{2,1,0:T(8,128)S(1)} %collective-permute-done.16), channel_id=1, source_target_pairs={{0,1},{1,2},{2,3},{3,4},{4,5},{5,6},{6,7},{7,8},{8,9},{9,10},{10,1... | collective-permute-start | bytes 98312 | tf_op jit(solution)/shard_map/ppermute | solution.py:93
  210.4 7.1 %collective-permute-start.19 = (f32[4,16,128]{2,1,0:T(8,128)S(1)}, f32[4,16,128]{2,1,0:T(8,128)S(1)}, u32[]{:S(2)}, u32[]{:S(2)}) collective-permute-start(f32[4,16,128]{2,1,0:T(8,128)S(1)} %collective-permute-done.17), channel_id=1, source_target_pairs={{0,15},{1,0},{2,1},{3,2},{4,3},{5,4},{6,5},{7,6},{8,7},{9,8},{10,9... | collective-permute-start | bytes 98312 | tf_op jit(solution)/shard_map/ppermute | solution.py:101
  215.5 7.0 %collective-permute-start.20 = (f32[4,16,128]{2,1,0:T(8,128)S(1)}, f32[4,16,128]{2,1,0:T(8,128)S(1)}, u32[]{:S(2)}, u32[]{:S(2)}) collective-permute-start(f32[4,16,128]{2,1,0:T(8,128)S(1)} %collective-permute-done.18), channel_id=1, source_target_pairs={{0,1},{1,2},{2,3},{3,4},{4,5},{5,6},{6,7},{7,8},{8,9},{9,10},{10,1... | collective-permute-start | bytes 98312 | tf_op jit(solution)/shard_map/ppermute | solution.py:93
  217.5 5.0 %copy-start.2 = (f32[4,256,128]{2,1,0:T(8,128)}, f32[4,256,128]{2,1,0:T(8,128)S(1)}, u32[]{:S(2)}) copy-start(f32[4,256,128]{2,1,0:T(8,128)S(1)} %constant_dynamic-update-slice_fusion.1) | copy-start | bytes 1572868
